TPU v7x, 512 devices: a whole 4x8x8 slice. The times are simulated.
512 devices in a mesh: rep: 32 (over x, y_hi, core), fsdp: 16 (over y_lo, z).
Axes of the slice: x: 4, y: 8 (y_hi: 4, y_lo: 2; y = y_hi * 2 + y_lo), z: 8, core: 2. Of those that a mesh axis runs over, the one named last changes fastest.
Arguments:
- tokens: bfloat16 [32, 2048, 8192], P('rep', 'fsdp'), may hold values from -6 to 6
- norm_gain: float32 [8192], replicated, may hold values from 0.25 to 3
- weights: bfloat16 [32, 8192, 512], P('rep', 'fsdp'), may hold values from -0.0625 to 0.0625
- first_moment: bfloat16 [32, 8192, 512], P('rep', 'fsdp'), may hold values from -0.0078125 to 0.0078125
- second_moment: bfloat16 [32, 8192, 512], P('rep', 'fsdp'), may hold values from 9.9651515e-08 to 9.983778e-07
- upstream: bfloat16 [32, 2048, 512], P('rep', 'fsdp'), may hold values from -6 to 6
- global_params: float32 [4, 16, 512, 128], P(None, 'fsdp', 'rep'), may hold values from -0.0625 to 0.0625
- outer_momentum: float32 [4, 16, 512, 128], P(None, 'fsdp', 'rep'), may hold values from -0.078125 to 0.078125
- fragment: int32 [1], replicated, may hold values from 0 to 3
Outputs:
- new_weights: bfloat16 [32, 8192, 512], P('rep', 'fsdp')
- values: bfloat16 [32, 2048, 512], P('rep', 'fsdp')
- new_global: float32 [4, 16, 512, 128], P(None, 'fsdp', 'rep')
- new_momentum: float32 [4, 16, 512, 128], P(None, 'fsdp', 'rep')
All inputs are finite; a program needn't handle non-finite values.
Results may differ from a plain program's by a relative error of at most 0.0049.
Values may be sent and summed in bfloat16 or wider, within the bound.
A program may use at most 64 MiB of HBM per device.

v0:
```python
import jax
import jax.numpy as jnp
from jax import lax
from jax.sharding import PartitionSpec as P

clip_bound = 1.0
inner_rate = 0.02
decay_rate = 0.1
outer_rate = 0.7
outer_mom = 0.9
blend = 0.5


def per_device(
    tokens,
    norm_gain,
    weights,
    first_moment,
    second_moment,
    upstream,
    global_params,
    outer_momentum,
    fragment,
):
    xf = tokens[0].astype(jnp.float32)
    scale = lax.rsqrt(jnp.mean(xf * xf, axis=-1, keepdims=True) + 1e-05)
    normed = (xf * scale * norm_gain).astype(jnp.bfloat16)
    w_local = weights[0]
    columns = lax.all_to_all(normed, "fsdp", split_axis=1, concat_axis=0, tiled=True)
    block = normed
    summed_values = jnp.dot(
        block,
        lax.all_gather(w_local, "fsdp", axis=0, tiled=True),
        preferred_element_type=jnp.float32,
    )
    block = columns
    grad = lax.dot_general(
        block,
        lax.all_gather(upstream[0], "fsdp", axis=0, tiled=True),
        (((0,), (0,)), ((), ())),
        preferred_element_type=jnp.float32,
    )
    total = lax.psum(jnp.sum(grad * grad), "fsdp")
    factor = jnp.minimum(1.0, clip_bound / (jnp.sqrt(total) + 1e-06))
    clipped = factor * grad
    moment = 0.9 * first_moment[0].astype(jnp.float32) + 0.1 * clipped
    square = 0.95 * second_moment[0].astype(jnp.float32) + 0.05 * clipped * clipped
    wf = w_local.astype(jnp.float32)
    inner = wf - inner_rate * (moment / (jnp.sqrt(square) + 1e-08) + decay_rate * wf)
    frag = fragment[0]
    head_size = global_params.shape[-1]
    start_col = frag * head_size
    share_rows = global_params.shape[2]
    replicas = lax.axis_size("rep")
    rank = lax.axis_index("rep")
    share_global = lax.dynamic_index_in_dim(global_params, frag, 0, keepdims=False)[0]
    share_moment = lax.dynamic_index_in_dim(outer_momentum, frag, 0, keepdims=False)[0]
    old_cols = lax.dynamic_slice_in_dim(wf, start_col, head_size, 1)
    summed = lax.psum(old_cols.astype(jnp.bfloat16), "rep").astype(jnp.float32)
    own_sum = lax.dynamic_slice_in_dim(summed, rank * share_rows, share_rows, 0)
    delta = share_global - own_sum / replicas
    moment_new = outer_mom * share_moment + delta
    global_new = share_global - outer_rate * (outer_mom * moment_new + delta)
    global_rows = lax.all_gather(global_new, "rep", axis=0, tiled=True)
    merged = (
        blend * lax.dynamic_slice_in_dim(inner, start_col, head_size, 1)
        + (1.0 - blend) * global_rows
    )
    new_local = lax.dynamic_update_slice_in_dim(inner, merged, start_col, 1).astype(jnp.bfloat16)
    frag_mask = (jnp.arange(global_params.shape[0]) == frag)[:, None, None, None]
    new_global = jnp.where(frag_mask, global_new[None, None], global_params)
    new_momentum = jnp.where(frag_mask, moment_new[None, None], outer_momentum)
    return (new_local[None], summed_values.astype(jnp.bfloat16)[None], new_global, new_momentum)


def solution(mesh):
    placed = (
        P("rep", "fsdp", None),
        P(),
        P("rep", "fsdp", None),
        P("rep", "fsdp", None),
        P("rep", "fsdp", None),
        P("rep", "fsdp", None),
        P(None, "fsdp", "rep", None),
        P(None, "fsdp", "rep", None),
        P(),
    )
    return jax.shard_map(
        per_device,
        mesh=mesh,
        in_specs=placed,
        out_specs=(
            P("rep", "fsdp", None),
            P("rep", "fsdp", None),
            P(None, "fsdp", "rep", None),
            P(None, "fsdp", "rep", None),
        ),
        check_vma=False,
    )
```

profile of v0, /device:TPU:1, one launch (start us, length us, event | category | flops | bytes accessed | tf_op | source)
XLA Modules:
  0.0 405.5 jit_solution(16264492084059616416)
XLA Ops:
  8.0 0.0 all-reduce.2.cloned.1.call-start
  8.7 1.6 fusion.28
  10.3 0.0 all-reduce.2.cloned.1.call-update
  10.3 0.0 all-gather.5.cloned.1.call-start
  10.3 0.5 all-gather.5.cloned.1.call-update
  10.9 0.0 all-gather.7.cloned.1.call-start
  10.9 0.5 all-gather.7.cloned.1.call-update
  11.5 0.8 mul.110
  12.2 3.2 copy.13
  15.4 1.1 fusion.2
  16.6 2.2 multiply_convert_fusion
  18.8 0.0 copy-start.3
  18.8 0.0 copy-start.4
  18.8 12.2 %all-to-all-start = ((bf16[128,16,512]{0,2,1:T(8,128)(2,1)}), bf16[128,16,512]{0,2,1:T(8,128)(2,1)}, u32[]{:S(2)}, u32[]{:S(2)}) async-start(bf16[128,16,512]{0,2,1:T(8,128)(2,1)} %multiply_convert_fusion), calls=%async_computation | async-start | bytes 4194304 | tf_op jit(solution)/shard_map/all_to_all | solution.py:29
  31.0 262.6 %all-reduce.2.cloned.1.call-done = bf16[512,128]{1,0:T(8,128)(2,1)} async-done(((bf16[512,128]{1,0:T(8,128)(2,1)}), bf16[512,128]{1,0:T(8,128)(2,1)}) %all-reduce.2.cloned.1.call-update) | async-done | bytes 131088 | tf_op jit(solution)/shard_map/psum | solution.py:59
  293.6 0.0 copy-done.3
  293.6 0.0 copy-done.4
  293.6 0.7 bitcast_subtract_fusion
  294.3 42.3 %all_gather.10 = f32[512,128]{1,0:T(8,128)S(1)} all-gather(f32[16,128]{1,0:T(8,128)S(1)} %get-tuple-element.4), channel_id=1, replica_groups=mesh['rep'=32,'fsdp'=16] {'rep'}, dimensions={0}, use_global_device_ids=true | all-gather | bytes 270336 | tf_op jit(solution)/shard_map/all_gather | solution.py:64
  336.6 0.7 broadcast_select_fusion
  337.3 0.0 all-to-all-done
  337.3 3.9 copy.14
  341.2 0.0 all-gather.5.cloned.1.call-done
  341.2 0.0 copy-start
  341.2 0.0 copy-start.1
  341.2 5.2 %multiply_reduce_fusion = (f32[]{:T(128)}, f32[512,512]{1,0:T(8,128)}) fusion(bf16[2048,512]{1,0:T(8,128)(2,1)} %bitcast.66, bf16[1,2048,512]{2,1,0:T(8,128)(2,1)} %all-gather.5.cloned.1.call-done), kind=kOutput, calls=%fused_computation.25 | convolution fusion | flops 1074266112 | bytes 5242884 | tf_op jit(solution)/shard_map/dot_general | solution.py:37
  346.4 40.3 %psum.14 = f32[]{:T(128)} all-reduce(f32[]{:T(128)} %get-tuple-element.8), channel_id=1, replica_groups=mesh['rep'=32,'fsdp'=16] {'fsdp'}, use_global_device_ids=true, to_apply=%region_2.0 | all-reduce | flops 1 | bytes 8 | tf_op jit(solution)/shard_map/psum | solution.py:43
  387.4 0.0 copy-done
  387.4 0.0 copy-done.1
  387.5 2.2 fusion.27
  389.7 0.0 copy-start.2
  389.7 0.1 multiply_dynamic-update-slice_fusion
  389.8 0.9 convert_bitcast_fusion
  390.6 0.0 all-gather.7.cloned.1.call-done
  390.6 0.0 copy-done.2
  390.6 7.5 %fusion.16 = bf16[1,128,512]{2,1,0:T(8,128)(2,1)} fusion(bf16[1,8192,512]{2,1,0:T(8,128)(2,1)} %all-gather.7.cloned.1.call-done, bf16[1,128,8192]{1,2,0:T(8,128)(2,1)S(1)} %copy.13, f32[8192]{0:T(1024)S(1)} %copy-done.2, f32[128]{0:T(128)S(1)} %add_rsqrt_fusion), kind=kOutput, calls=%fused_computation.15 | convolution fusion | flops 1078001664 | bytes 10650112 | tf_op jit(solution)/shard_map/dot_general | solution.py:31
  (2 shorter events, 0.0 us)
Async XLA Ops:
  8.0 285.6 %all-reduce.2.cloned.1.call-start = ((), (), s32[]{:S(2)}) async-start(), calls=%async_computation.1 | async-start | bytes 262144 | tf_op jit(solution)/shard_map/psum | solution.py:59
  10.3 330.9 %all-gather.5.cloned.1.call-start = ((), (), s32[]{:S(2)}) async-start(), calls=%async_computation.2 | async-start | bytes 2228224 | tf_op jit(solution)/shard_map/all_gather | solution.py:39
  10.9 379.8 %all-gather.7.cloned.1.call-start = ((), (), s32[]{:S(2)}) async-start(), calls=%async_computation.3 | async-start | bytes 8912896 | tf_op jit(solution)/shard_map/all_gather | solution.py:33
  18.8 274.8 %copy-start.3 = (f32[4,1,16,128]{3,2,1,0:T(8,128)S(1)}, f32[4,1,16,128]{3,2,1,0:T(8,128)}, u32[]{:S(2)}) copy-start(f32[4,1,16,128]{3,2,1,0:T(8,128)} %param.15) | copy-start | bytes 98308
  18.8 274.8 %copy-start.4 = (f32[4,1,16,128]{3,2,1,0:T(8,128)S(1)}, f32[4,1,16,128]{3,2,1,0:T(8,128)}, u32[]{:S(2)}) copy-start(f32[4,1,16,128]{3,2,1,0:T(8,128)} %param.16) | copy-start | bytes 98308
  18.8 318.5 %all-to-all-start = ((bf16[128,16,512]{0,2,1:T(8,128)(2,1)}), bf16[128,16,512]{0,2,1:T(8,128)(2,1)}, u32[]{:S(2)}, u32[]{:S(2)}) async-start(bf16[128,16,512]{0,2,1:T(8,128)(2,1)} %multiply_convert_fusion), calls=%async_computation | async-start | bytes 4194304 | tf_op jit(solution)/shard_map/all_to_all | solution.py:29
  341.2 46.2 %copy-start = (bf16[1,512,512]{2,1,0:T(8,128)(2,1)S(1)}, bf16[1,512,512]{2,1,0:T(8,128)(2,1)}, u32[]{:S(2)}) copy-start(bf16[1,512,512]{2,1,0:T(8,128)(2,1)} %param.11) | copy-start | bytes 1572868
  341.2 46.2 %copy-start.1 = (bf16[1,512,512]{2,1,0:T(8,128)(2,1)S(1)}, bf16[1,512,512]{2,1,0:T(8,128)(2,1)}, u32[]{:S(2)}) copy-start(bf16[1,512,512]{2,1,0:T(8,128)(2,1)} %param.13) | copy-start | bytes 1572868
  389.7 1.0 copy-start.2
Sparse Core Ops, SparseCore 0:
  12.3 281.2 all-reduce.1
Sparse Core Ops, SparseCore 1:
  12.8 111.4 all-gather.4
  126.5 110.7 all-gather.6
where the time goes:
time: 412 us; the launch traced here: 406 us
  waiting for transfers between devices  264 us (64%)
  blocking collectives  82.6 us (20%)
  between operations  16.9 us (4%)
  matrix products  12.7 us (3%)
  starting transfers between devices  12.3 us (3%)
  local copies, waits for them, and re-layouts  9.47 us (2%)
  other arithmetic  7.88 us (2%)
    psum x1, waiting for transfers between devices, per_device(): summed = lax.psum(old_cols.astype(jnp.bfloat16), 'rep').astype(jnp.float32)  263 us
    all_gather x1, blocking collectives, per_device(): global_rows = lax.all_gather(global_new, 'rep', axis=0, tiled=True)  42.3 us
    psum x1, blocking collectives, per_device(): total = lax.psum(jnp.sum(grad * grad), 'fsdp')  40.3 us
    all_to_all x1, starting transfers between devices, per_device(): lax.all_to_all(normed, 'fsdp', split_axis=1, concat_axis=0, tiled=True)  12.2 us
  transfers between devices with their start and end apart: 4, of which 1 were waited for; matrix products, arithmetic and copies ran while one was open for 5% of the time, Pallas kernels for 0%

commit v1 on v0

v1 whole, which is shorter than its diff:
```python
import functools

import jax
import jax.numpy as jnp
from jax import lax
from jax.experimental import pallas as pl
from jax.experimental.pallas import tpu as pltpu
from jax.sharding import PartitionSpec as P

MESH = pl.DeviceIdType.MESH

clip_bound = 1.0
inner_rate = 0.02
decay_rate = 0.1
outer_rate = 0.7
outer_mom = 0.9
blend = 0.5

ORDER = (1, 7, 2, 6, 3, 5, 4)


def kernel(
    n_rep,
    nz,
    tok_hbm,
    gain_ref,
    w_hbm,
    fm_hbm,
    sm_hbm,
    u_hbm,
    gp_ref,
    mom_ref,
    frag_ref,
    nw_hbm,
    val_hbm,
    ng_ref,
    nm_ref,
    x,
    tp,
    to,
    tg,
    wcat,
    ucat,
    fm,
    sm,
    nw,
    gown,
    gsend,
    grecv,
    vsend,
    vrecv,
    vown,
    vout,
    scale_ref,
    wsel,
    wrecv,
    gnew,
    grow,
    gfull,
    nsend,
    nrecv,
    loc,
    t_s,
    t_r,
    u_s,
    u_r,
    v_s,
    v_r,
    one_s,
    one_r,
):
    r = lax.axis_index("rep")
    f = lax.axis_index("fsdp")
    y, z = f // nz, f % nz
    n_f = 2 * nz
    partner = (1 - y) * nz + z
    rows, feats = 128, 512
    peers = ORDER

    def zdev(k):
        return {"rep": r, "fsdp": y * nz + (z + k) % nz}

    barrier = pltpu.get_barrier_semaphore()

    def greet_f(k, c):
        pl.semaphore_signal(barrier, inc=1, device_id={"rep": r, "fsdp": (f + k) % n_f}, device_id_type=MESH)
        return c

    def greet_r(k, c):
        pl.semaphore_signal(barrier, inc=1, device_id={"rep": (r + k) % n_rep, "fsdp": f}, device_id_type=MESH)
        return c

    lax.fori_loop(1, n_f, greet_f, 0)
    lax.fori_loop(1, n_rep, greet_r, 0)

    local = [
        pltpu.make_async_copy(tok_hbm, x, loc.at[0]),
        pltpu.make_async_copy(w_hbm, wcat.at[pl.ds(feats, feats), :], loc.at[1]),
        pltpu.make_async_copy(u_hbm, ucat.at[0], loc.at[2]),
        pltpu.make_async_copy(fm_hbm, fm, loc.at[3]),
        pltpu.make_async_copy(sm_hbm, sm, loc.at[4]),
    ]
    for c in local:
        c.start()

    frag = frag_ref[0]
    local[1].wait()
    sel = wcat[pl.ds(feats, feats), 0:128]
    for j in range(1, 4):
        sel = jnp.where(frag == j, wcat[pl.ds(feats, feats), j * 128 : (j + 1) * 128], sel)
    wsel[...] = sel.reshape(wsel.shape)

    local[0].wait()

    def squares(i, acc):
        for j in range(4):
            v = x[:, pl.ds(pl.multiple_of(i * 512 + j * 128, 128), 128)].astype(jnp.float32)
            acc = acc + v * v
        return acc

    acc = lax.fori_loop(0, 16, squares, jnp.zeros((rows, 128), jnp.float32))
    mean = jnp.sum(acc, axis=1, keepdims=True) / (16 * feats)
    scale_ref[...] = jnp.broadcast_to(lax.rsqrt(mean + 1e-05), (rows, 128))
    local[2].wait()
    for j in range(4):
        cols = slice(j * 128, (j + 1) * 128)
        ucat[0, :, cols] = (ucat[0, :, cols].astype(jnp.float32) * scale_ref[...]).astype(jnp.bfloat16)

    pl.semaphore_wait(barrier, n_f - 1 + n_rep - 1)

    w_copy = pltpu.make_async_remote_copy(
        src_ref=wcat.at[pl.ds(feats, feats), :],
        dst_ref=wcat.at[pl.ds(0, feats), :],
        send_sem=one_s.at[0],
        recv_sem=one_r.at[0],
        device_id={"rep": r, "fsdp": partner},
        device_id_type=MESH,
    )

    def send_rows(k, c):
        dst = (r + k) % n_rep
        pltpu.make_async_remote_copy(
            src_ref=wsel.at[dst],
            dst_ref=wrecv.at[k - 1],
            send_sem=one_s.at[1],
            recv_sem=one_r.at[1],
            device_id={"rep": dst, "fsdp": f},
            device_id_type=MESH,
        ).start()
        return c

    u_copies, p_copies, o_copies, v_copies = [], [], [], []
    for i, k in enumerate(peers):
        u_copies.append(
            pltpu.make_async_remote_copy(
                src_ref=ucat.at[0], dst_ref=ucat.at[i + 1], send_sem=u_s.at[i], recv_sem=u_r.at[i], device_id=zdev(k), device_id_type=MESH
            )
        )
        zk = (z + k) % nz
        for kind, dst, yk in ((0, tp, 1 - y), (1, to, y)):
            col = pl.multiple_of((yk * nz + zk) * feats, feats)
            (o_copies if kind else p_copies).append(
                pltpu.make_async_remote_copy(
                    src_ref=tok_hbm.at[:, pl.ds(col, feats)],
                    dst_ref=dst.at[i + 1],
                    send_sem=t_s.at[kind * 7 + i],
                    recv_sem=t_r.at[kind * 7 + i],
                    device_id=zdev(k),
                    device_id_type=MESH,
                )
            )
        v_copies.append(
            pltpu.make_async_remote_copy(
                src_ref=vsend.at[i], dst_ref=vrecv.at[i], send_sem=v_s.at[i], recv_sem=v_r.at[i], device_id=zdev(nz - k), device_id_type=MESH
            )
        )
    for c in u_copies:
        c.start()
    for c in p_copies[:4]:
        c.start()
    w_copy.start()
    lax.fori_loop(1, n_rep, send_rows, 0)
    for c in p_copies[4:]:
        c.start()
    for c in o_copies:
        c.start()

    def gained(src, i, kind, yk):
        first = (yk * nz + z) * 4
        at = pl.ds(pl.multiple_of(i * rows, rows), rows)
        for j in range(4):
            g = gain_ref[pl.ds(first + j, 1), :]
            v = src(j).astype(jnp.float32) * g
            tg[at, kind * feats + j * 128 : kind * feats + (j + 1) * 128] = v.astype(jnp.bfloat16)

    def own(yk):
        return lambda j: x[:, pl.ds(pl.multiple_of((yk * nz + z) * feats + j * 128, 128), 128)]

    def block(ref, i):
        return lambda j: ref[i, :, j * 128 : (j + 1) * 128]

    gained(own(1 - y), 0, 0, 1 - y)
    gained(own(y), 0, 1, y)

    pltpu.make_async_copy(wrecv, wrecv, one_r.at[1]).wait()

    def add_rows(k, acc):
        return acc + wrecv[k].astype(jnp.float32)

    total_rows = lax.fori_loop(0, n_rep - 1, add_rows, wsel[r].astype(jnp.float32))
    share_g, share_u = gp_ref[0, 0], mom_ref[0, 0]
    for j in range(1, 4):
        share_g = jnp.where(frag == j, gp_ref[j, 0], share_g)
        share_u = jnp.where(frag == j, mom_ref[j, 0], share_u)
    delta = share_g - total_rows / n_rep
    u_new = outer_mom * share_u + delta
    g_new = share_g - outer_rate * (outer_mom * u_new + delta)
    gnew[...] = g_new
    for j in range(4):
        ng_ref[j, 0] = jnp.where(frag == j, g_new, gp_ref[j, 0])
        nm_ref[j, 0] = jnp.where(frag == j, u_new, mom_ref[j, 0])

    def send_new(k, c):
        pltpu.make_async_remote_copy(
            src_ref=gnew,
            dst_ref=grow.at[k - 1],
            send_sem=one_s.at[2],
            recv_sem=one_r.at[2],
            device_id={"rep": (r + k) % n_rep, "fsdp": f},
            device_id_type=MESH,
        ).start()
        return c

    lax.fori_loop(1, n_rep, send_new, 0)

    for i in range(7):
        p_copies[i].wait_recv()
        gained(block(tp, i + 1), i + 1, 0, 1 - y)
    for c in u_copies:
        c.wait_recv()

    def grad(kind, m):
        cols = slice(kind * feats + m * 256, kind * feats + (m + 1) * 256)
        return lax.dot_general(
            tg[:, cols], ucat[...].reshape(nz * rows, feats), (((0,), (0,)), ((), ())), preferred_element_type=jnp.float32
        )

    for m in range(2):
        gsend[m * 256 : (m + 1) * 256, :] = grad(0, m).astype(jnp.bfloat16)
    g_copy = pltpu.make_async_remote_copy(
        src_ref=gsend,
        dst_ref=grecv,
        send_sem=one_s.at[3],
        recv_sem=one_r.at[3],
        device_id={"rep": r, "fsdp": partner},
        device_id_type=MESH,
    )
    g_copy.start()

    w_copy.wait_recv()
    vown[...] = jnp.dot(tg[0:rows, :], wcat[...], preferred_element_type=jnp.float32)

    pltpu.make_async_copy(grow, grow, one_r.at[2]).wait()
    gfull[r] = gnew[...]

    def place(k, c):
        gfull[(r + n_rep - k) % n_rep] = grow[k - 1]
        return c

    lax.fori_loop(1, n_rep, place, 0)

    for i in range(7):
        o_copies[i].wait_recv()
        gained(block(to, i + 1), i + 1, 1, y)
        at = slice((i + 1) * rows, (i + 2) * rows)
        vsend[i] = jnp.dot(tg[at, :], wcat[...], preferred_element_type=jnp.float32).astype(jnp.bfloat16)
        v_copies[i].start()

    g_copy.wait_recv()
    acc = jnp.zeros((8, feats), jnp.float32)
    for m in range(2):
        at = slice(m * 256, (m + 1) * 256)
        g = grad(1, m) + grecv[at, :].astype(jnp.float32)
        gown[at, :] = g
        acc = acc + jnp.sum((g * g).reshape(32, 8, feats), axis=0)
    nsend[...] = acc[:, 0:128] + acc[:, 128:256] + acc[:, 256:384] + acc[:, 384:512]

    def send_norm(k, c):
        pltpu.make_async_remote_copy(
            src_ref=nsend,
            dst_ref=nrecv.at[k - 1],
            send_sem=one_s.at[4],
            recv_sem=one_r.at[4],
            device_id={"rep": r, "fsdp": (f + k) % n_f},
            device_id_type=MESH,
        ).start()
        return c

    lax.fori_loop(1, n_f, send_norm, 0)
    local[3].wait()
    local[4].wait()
    pltpu.make_async_copy(nrecv, nrecv, one_r.at[4]).wait()
    tile = nsend[...] + jnp.sum(nrecv[...], axis=0)
    total = jnp.sum(jnp.sum(tile, axis=1, keepdims=True), axis=0, keepdims=True)
    factor = jnp.minimum(1.0, clip_bound / (jnp.sqrt(total) + 1e-06))

    def update(i, c):
        at = pl.ds(pl.multiple_of(i * 64, 64), 64)
        wat = pl.ds(pl.multiple_of(feats + i * 64, 64), 64)
        rows_new = gfull[pl.ds(i * 4, 4)].reshape(64, 128)
        for j in range(4):
            cols = slice(j * 128, (j + 1) * 128)
            clipped = gown[at, cols] * factor
            moment = 0.9 * fm[at, cols].astype(jnp.float32) + 0.1 * clipped
            square = 0.95 * sm[at, cols].astype(jnp.float32) + 0.05 * clipped * clipped
            wf = wcat[wat, cols].astype(jnp.float32)
            inner = wf - inner_rate * (moment / (jnp.sqrt(square) + 1e-08) + decay_rate * wf)
            merged = blend * inner + (1.0 - blend) * rows_new
            nw[at, cols] = jnp.where(frag == j, merged, inner).astype(jnp.bfloat16)
        return c

    lax.fori_loop(0, 8, update, 0)
    nw_copy = pltpu.make_async_copy(nw, nw_hbm, loc.at[5])
    nw_copy.start()

    for c in v_copies:
        c.wait_recv()
    for j in range(4):
        cols = slice(j * 128, (j + 1) * 128)
        acc = vown[:, cols]
        for i in range(7):
            acc = acc + vrecv[i, :, cols].astype(jnp.float32)
        vout[:, cols] = (acc * scale_ref[...]).astype(jnp.bfloat16)
    v_out = pltpu.make_async_copy(vout, val_hbm, loc.at[6])
    v_out.start()

    for c in u_copies + p_copies + o_copies + v_copies + [w_copy, g_copy]:
        c.wait_send()
    pltpu.make_async_copy(wrecv, wrecv, one_s.at[1]).wait()
    pltpu.make_async_copy(grow, grow, one_s.at[2]).wait()
    pltpu.make_async_copy(nrecv, nrecv, one_s.at[4]).wait()
    nw_copy.wait()
    v_out.wait()


def per_device(n_rep, n_fsdp, tokens, norm_gain, weights, first_moment, second_moment, upstream, global_params, outer_momentum, fragment):
    nz = n_fsdp // 2
    bf, f32 = jnp.bfloat16, jnp.float32
    vm, anywhere = pl.BlockSpec(memory_space=pltpu.VMEM), pl.BlockSpec(memory_space=pl.ANY)
    dma = pltpu.SemaphoreType.DMA
    out = pl.pallas_call(
        functools.partial(kernel, n_rep, nz),
        out_shape=(
            jax.ShapeDtypeStruct((512, 512), bf),
            jax.ShapeDtypeStruct((128, 512), bf),
            jax.ShapeDtypeStruct(global_params.shape, f32),
            jax.ShapeDtypeStruct(outer_momentum.shape, f32),
        ),
        in_specs=[anywhere, vm, anywhere, anywhere, anywhere, anywhere, vm, vm, pl.BlockSpec(memory_space=pltpu.SMEM)],
        out_specs=(anywhere, anywhere, vm, vm),
        scratch_shapes=[
            pltpu.VMEM((128, 8192), bf),
            pltpu.VMEM((8, 128, 512), bf),
            pltpu.VMEM((8, 128, 512), bf),
            pltpu.VMEM((1024, 1024), bf),
            pltpu.VMEM((1024, 512), bf),
            pltpu.VMEM((8, 128, 512), bf),
            pltpu.VMEM((512, 512), bf),
            pltpu.VMEM((512, 512), bf),
            pltpu.VMEM((512, 512), bf),
            pltpu.VMEM((512, 512), f32),
            pltpu.VMEM((512, 512), bf),
            pltpu.VMEM((512, 512), bf),
            pltpu.VMEM((7, 128, 512), bf),
            pltpu.VMEM((7, 128, 512), bf),
            pltpu.VMEM((128, 512), f32),
            pltpu.VMEM((128, 512), bf),
            pltpu.VMEM((128, 128), f32),
            pltpu.VMEM((n_rep, 16, 128), bf),
            pltpu.VMEM((n_rep - 1, 16, 128), bf),
            pltpu.VMEM((16, 128), f32),
            pltpu.VMEM((n_rep - 1, 16, 128), f32),
            pltpu.VMEM((n_rep, 16, 128), f32),
            pltpu.VMEM((8, 128), f32),
            pltpu.VMEM((n_fsdp - 1, 8, 128), f32),
            dma((7,)),
            dma((14,)),
            dma((14,)),
            dma((7,)),
            dma((7,)),
            dma((7,)),
            dma((7,)),
            dma((5,)),
            dma((5,)),
        ],
        compiler_params=pltpu.CompilerParams(collective_id=0, has_side_effects=True, vmem_limit_bytes=60 * 1024 * 1024),
        name="step",
    )(
        tokens[0],
        norm_gain.reshape(64, 128),
        weights[0],
        first_moment[0],
        second_moment[0],
        upstream[0],
        global_params,
        outer_momentum,
        fragment,
    )
    return (out[0][None], out[1][None], out[2], out[3])


def solution(mesh):
    placed = (
        P("rep", "fsdp", None),
        P(),
        P("rep", "fsdp", None),
        P("rep", "fsdp", None),
        P("rep", "fsdp", None),
        P("rep", "fsdp", None),
        P(None, "fsdp", "rep", None),
        P(None, "fsdp", "rep", None),
        P(),
    )
    return jax.shard_map(
        functools.partial(per_device, mesh.shape["rep"], mesh.shape["fsdp"]),
        mesh=mesh,
        in_specs=placed,
        out_specs=(
            P("rep", "fsdp", None),
            P("rep", "fsdp", None),
            P(None, "fsdp", "rep", None),
            P(None, "fsdp", "rep", None),
        ),
        check_vma=False,
    )
```

time: 412 us -> 123 us (0.30); the launches traced: 406 us -> 123 us
  waiting for transfers between devices: 264 us -> 0 us
  Pallas kernels: 0 us -> 115 us
  blocking collectives: 82.6 us -> 0 us
  between operations: 16.9 us -> 1.29 us
  matrix products: 12.7 us -> 0 us
  starting transfers between devices: 12.3 us -> 0 us
  other arithmetic: 7.88 us -> 0 us
    psum x1 -> x0, waiting for transfers between devices: 263 us -> none  [per_device(): summed = lax.psum(old_cols.astype(jnp.bfloat16), 'rep').astype(jnp.float32)]
    pallas_call x0 -> x1, Pallas kernels: none -> 115 us  [per_device(): pl.pallas_call(functools.partial(kernel, n_rep, nz), out_shape=(jax.Shape...]
    all_gather x1 -> x0, blocking collectives: 42.3 us -> none  [per_device(): global_rows = lax.all_gather(global_new, 'rep', axis=0, tiled=True)]
    psum x1 -> x0, blocking collectives: 40.3 us -> none  [per_device(): total = lax.psum(jnp.sum(grad * grad), 'fsdp')]
    dot_general x2 -> x0, matrix products: 12.7 us -> none  [the longest x1 7.48 us: per_device(): jnp.dot(block, lax.all_gather(w_local, 'fsdp', axis=0, tiled=True), prefe...]
    all_to_all x1 -> x0, starting transfers between devices: 12.2 us -> none  [per_device(): lax.all_to_all(normed, 'fsdp', split_axis=1, concat_axis=0, tiled=True)]
  transfers between devices with their start and end apart: 4 -> 0, of which waited for: 1 -> 0; matrix products, arithmetic and copies ran while one was open for 5% -> 0% of each run, Pallas kernels for 0% -> 0%
where the time goes in v1:
time: 123 us
  Pallas kernels  115 us (93%)
  local copies, waits for them, and re-layouts  6.18 us (5%)
  between operations  1.29 us (1%)
    pallas_call x1, Pallas kernels, per_device(): pl.pallas_call(functools.partial(kernel, n_rep, nz), out_shape=(jax.Shape...  115 us
    unnamed x4, local copies, waits for them, and re-layouts  6.18 us

profile of v1, /device:TPU:1, one launch (start us, length us, event | category | flops | bytes accessed | tf_op | source)
XLA Modules:
  0.0 122.7 jit_solution(15544581289072237504)
XLA Ops:
  1.3 115.2 %step.1 = (bf16[512,512]{1,0:T(8,128)(2,1)}, bf16[128,512]{1,0:T(8,128)(2,1)}, f32[4,1,16,128]{3,2,1,0:T(8,128)}, f32[4,1,16,128]{3,2,1,0:T(8,128)}) custom-call(bf16[128,8192]{1,0:T(8,128)(2,1)} %bitcast.8, f32[64,128]{1,0:T(8,128)} %bitcast.15, bf16[512,512]{1,0:T(8,128)(2,1)} %bitcast.9, bf16[512,512]{1,0:T(8,128)(2,1)} %bitcast.10, ...), custom_call_target="tpu_custom_call" | custom-call | tf_op jit(solution)/shard_map/step/pallas_call | solution.py:351
  116.5 1.9 %copy.18 = bf16[1,512,512]{2,1,0:T(8,128)(2,1)} copy(bf16[1,512,512]{2,1,0:T(8,128)(2,1)} %bitcast.12) | data formatting | bytes 1048576
  118.4 1.6 %copy.19 = bf16[1,128,512]{2,1,0:T(8,128)(2,1)} copy(bf16[1,128,512]{2,1,0:T(8,128)(2,1)} %bitcast.14) | data formatting | bytes 262144
  119.9 1.4 %copy.20 = f32[4,1,16,128]{3,2,1,0:T(8,128)} copy(f32[4,1,16,128]{3,2,1,0:T(8,128)} %get-tuple-element.18) | data formatting | bytes 65536
  121.3 1.4 %copy.21 = f32[4,1,16,128]{3,2,1,0:T(8,128)} copy(f32[4,1,16,128]{3,2,1,0:T(8,128)} %get-tuple-element.19) | data formatting | bytes 65536

commit v2 on v1

v2 whole, which is shorter than its diff:
```python
import functools

import jax
import jax.numpy as jnp
from jax import lax
from jax.experimental import pallas as pl
from jax.experimental.pallas import tpu as pltpu
from jax.sharding import PartitionSpec as P

MESH = pl.DeviceIdType.MESH

clip_bound = 1.0
inner_rate = 0.02
decay_rate = 0.1
outer_rate = 0.7
outer_mom = 0.9
blend = 0.5

ORDER = (1, 7, 2, 6, 3, 5, 4)
AHEAD, BACK = (0, 1, 3, 5, 7), (0, 2, 4, 6, 7)
FAR = (7, 5, 6, 3, 4, 1, 2)


def kernel(
    n_rep,
    nz,
    tok_hbm,
    gain_ref,
    w_hbm,
    fm_hbm,
    sm_hbm,
    u_hbm,
    gp_ref,
    mom_ref,
    frag_ref,
    nw_hbm,
    val_hbm,
    ng_ref,
    nm_ref,
    x,
    xn,
    tp,
    to,
    w,
    wp,
    u,
    fm,
    sm,
    nw,
    gown,
    gsend,
    grecv,
    vsend,
    vrecv,
    vown,
    vout,
    scale_ref,
    wsel,
    wrecv,
    gnew,
    grow,
    gfull,
    nsend,
    nrecv,
    loc,
    t_s,
    t_r,
    u_s,
    u_r,
    v_s,
    v_r,
    one_s,
    one_r,
):
    r = lax.axis_index("rep")
    f = lax.axis_index("fsdp")
    y, z = f // nz, f % nz
    n_f = 2 * nz
    rows, feats = 128, 512
    f32, bf16 = jnp.float32, jnp.bfloat16

    def zdev(k):
        return {"rep": r, "fsdp": y * nz + (z + k) % nz}

    partner = {"rep": r, "fsdp": (1 - y) * nz + z}

    def remote(src, dst, send_sem, recv_sem, device):
        return pltpu.make_async_remote_copy(
            src_ref=src, dst_ref=dst, send_sem=send_sem, recv_sem=recv_sem, device_id=device, device_id_type=MESH
        )

    barrier = pltpu.get_barrier_semaphore()

    def greet_f(k, c):
        pl.semaphore_signal(barrier, inc=1, device_id={"rep": r, "fsdp": (f + k) % n_f}, device_id_type=MESH)
        return c

    def greet_r(k, c):
        pl.semaphore_signal(barrier, inc=1, device_id={"rep": (r + k) % n_rep, "fsdp": f}, device_id_type=MESH)
        return c

    local = [
        pltpu.make_async_copy(tok_hbm, x, loc.at[0]),
        pltpu.make_async_copy(w_hbm, w, loc.at[1]),
        pltpu.make_async_copy(u_hbm, u.at[0], loc.at[2]),
        pltpu.make_async_copy(fm_hbm, fm, loc.at[3]),
        pltpu.make_async_copy(sm_hbm, sm, loc.at[4]),
    ]
    for c in local:
        c.start()
    lax.fori_loop(1, n_f, greet_f, 0)
    lax.fori_loop(1, n_rep, greet_r, 0)

    frag = frag_ref[0]
    local[0].wait()

    def squares(i, acc):
        for j in range(4):
            v = x[:, pl.ds(pl.multiple_of(i * 512 + j * 128, 128), 128)].astype(f32)
            acc = acc + v * v
        return acc

    acc = lax.fori_loop(0, 2 * nz, squares, jnp.zeros((rows, 128), f32))
    mean = jnp.sum(acc, axis=1, keepdims=True) / (2 * nz * feats)
    scale_ref[...] = jnp.broadcast_to(lax.rsqrt(mean + 1e-05), (rows, 128))

    def normed(block, dst):
        for j in range(4):
            g = gain_ref[pl.ds(block * 4 + j, 1), :]
            v = x[:, pl.ds(pl.multiple_of(block * feats + j * 128, 128), 128)].astype(f32)
            dst[:, j * 128 : (j + 1) * 128] = (v * scale_ref[...] * g).astype(bf16)

    copies = []

    def keep(c):
        c.start()
        copies.append(c)
        return c

    t_in = {}

    def prepare(kind, i):
        block = (1 - y if kind == 0 else y) * nz + (z + ORDER[i - 1]) % nz
        normed(block, xn.at[kind * 7 + i - 1])

    def send_tokens(kind, i):
        n = kind * 7 + i - 1
        t_in[kind, i] = keep(remote(xn.at[n], (to if kind else tp).at[i], t_s.at[n], t_r.at[n], zdev(ORDER[i - 1])))

    for i in FAR[:3]:
        prepare(0, i)
    local[1].wait()
    sel = w[:, 0:128]
    for j in range(1, 4):
        sel = jnp.where(frag == j, w[:, j * 128 : (j + 1) * 128], sel)
    wsel[...] = sel.reshape(wsel.shape)
    local[2].wait()

    pl.semaphore_wait(barrier, n_f - 1 + n_rep - 1)

    def hop(h):
        part = [slice(0, rows), slice(0, rows)] if h < 4 else [slice(0, rows // 2), slice(rows // 2, rows)]
        return [
            keep(remote(u.at[s[h - 1], p], u.at[s[h], p], u_s.at[2 * h - 2 + n], u_r.at[2 * h - 2 + n], zdev((1, nz - 1)[n])))
            for n, (s, p) in enumerate(zip((AHEAD, BACK), part))
        ]

    u_in = hop(1)
    for i in FAR[:3]:
        send_tokens(0, i)
    w_copy = keep(remote(w, wp, one_s.at[0], one_r.at[0], partner))

    def send_rows(k, c):
        dst = (r + k) % n_rep
        remote(wsel.at[dst], wrecv.at[k - 1], one_s.at[1], one_r.at[1], {"rep": dst, "fsdp": f}).start()
        return c

    lax.fori_loop(1, n_rep, send_rows, 0)
    for i in FAR[3:]:
        prepare(0, i)

    for c in u_in:
        c.wait_recv()
    u_in = hop(2)
    for i in FAR[3:5]:
        send_tokens(0, i)
    normed((1 - y) * nz + z, tp.at[0])
    normed(y * nz + z, to.at[0])
    for c in u_in:
        c.wait_recv()
    u_in = hop(3)
    for i in FAR[5:]:
        send_tokens(0, i)
    for i in FAR:
        prepare(1, i)

    pltpu.make_async_copy(wrecv, wrecv, one_r.at[1]).wait()

    def add_rows(k, acc):
        return acc + wrecv[k].astype(f32)

    total_rows = lax.fori_loop(0, n_rep - 1, add_rows, wsel[r].astype(f32))
    share_g, share_u = gp_ref[0, 0], mom_ref[0, 0]
    for j in range(1, 4):
        share_g = jnp.where(frag == j, gp_ref[j, 0], share_g)
        share_u = jnp.where(frag == j, mom_ref[j, 0], share_u)
    delta = share_g - total_rows / n_rep
    u_new = outer_mom * share_u + delta
    g_new = share_g - outer_rate * (outer_mom * u_new + delta)
    gnew[...] = g_new

    def send_new(k, c):
        remote(gnew, grow.at[k - 1], one_s.at[2], one_r.at[2], {"rep": (r + k) % n_rep, "fsdp": f}).start()
        return c

    for c in u_in:
        c.wait_recv()
    u_in = hop(4)
    for i in FAR:
        send_tokens(1, i)
    lax.fori_loop(1, n_rep, send_new, 0)
    for j in range(4):
        ng_ref[j, 0] = jnp.where(frag == j, g_new, gp_ref[j, 0])
        nm_ref[j, 0] = jnp.where(frag == j, u_new, mom_ref[j, 0])

    def grad(t, first, count, cols):
        k = count * rows
        return lax.dot_general(
            t[first : first + count, :, cols].reshape(k, -1),
            u[first : first + count].reshape(k, feats),
            (((0,), (0,)), ((), ())),
            preferred_element_type=f32,
        )

    for i in FAR:
        t_in[0, i].wait_recv()
    for c in u_in:
        c.wait_recv()
    halves = (slice(0, 256), slice(256, 512))
    for m in halves:
        gsend[m, :] = grad(tp, 0, nz, m).astype(bf16)
    g_copy = keep(remote(gsend, grecv, one_s.at[3], one_r.at[3], partner))

    w_copy.wait_recv()

    def partial(i):
        return jnp.dot(tp[i], wp[...], preferred_element_type=f32) + jnp.dot(to[i], w[...], preferred_element_type=f32)

    vown[...] = partial(0)

    t_in[1, 7].wait_recv()
    vsend[0] = partial(7).astype(bf16)
    first_half, last_half = slice(0, rows // 2), slice(rows // 2, rows)
    v_in = [
        keep(remote(vsend.at[0, p], vrecv.at[0, p], v_s.at[n], v_r.at[n], zdev((1, nz - 1)[n])))
        for n, p in enumerate((first_half, last_half))
    ]
    for m in halves:
        gown[m, :] = grad(to, 0, 1, m) + grad(to, 7, 1, m)

    pltpu.make_async_copy(grow, grow, one_r.at[2]).wait()
    gfull[r] = gnew[...]

    def place(k, c):
        gfull[(r + n_rep - k) % n_rep] = grow[k - 1]
        return c

    lax.fori_loop(1, n_rep, place, 0)

    for s in (2, 3):
        a, b = {2: (6, 5), 3: (4, 3)}[s]
        at = 2 * s - 2
        t_in[1, a].wait_recv()
        ahead = partial(a)
        t_in[1, b].wait_recv()
        back = partial(b)
        v_in[0].wait_recv()
        if s == 2:
            vsend[at, first_half] = (ahead[first_half] + vrecv[0, first_half].astype(f32)).astype(bf16)
            vsend[at, last_half] = ahead[last_half].astype(bf16)
        else:
            vsend[at] = (ahead + vrecv[at - 2].astype(f32)).astype(bf16)
        ahead_copy = keep(remote(vsend.at[at], vrecv.at[at], v_s.at[at], v_r.at[at], zdev(1)))
        v_in[1].wait_recv()
        if s == 2:
            vsend[at + 1, last_half] = (back[last_half] + vrecv[0, last_half].astype(f32)).astype(bf16)
            vsend[at + 1, first_half] = back[first_half].astype(bf16)
        else:
            vsend[at + 1] = (back + vrecv[at - 1].astype(f32)).astype(bf16)
        back_copy = keep(remote(vsend.at[at + 1], vrecv.at[at + 1], v_s.at[at + 1], v_r.at[at + 1], zdev(nz - 1)))
        v_in = [ahead_copy, back_copy]
        for m in halves:
            gown[m, :] += grad(to, b, 2, m)

    g_copy.wait_recv()
    t_in[1, 1].wait_recv()
    t_in[1, 2].wait_recv()
    acc = jnp.zeros((8, feats), f32)
    for m in halves:
        g = gown[m, :] + grecv[m, :].astype(f32) + grad(to, 1, 2, m)
        gown[m, :] = g
        acc = acc + jnp.sum((g * g).reshape(32, 8, feats), axis=0)
    nsend[...] = acc[:, 0:128] + acc[:, 128:256] + acc[:, 256:384] + acc[:, 384:512]

    def send_norm(k, c):
        remote(nsend, nrecv.at[k - 1], one_s.at[4], one_r.at[4], {"rep": r, "fsdp": (f + k) % n_f}).start()
        return c

    lax.fori_loop(1, n_f, send_norm, 0)

    ahead, back = partial(2), partial(1)
    v_in[0].wait_recv()
    vsend[6] = (ahead + vrecv[4].astype(f32)).astype(bf16)
    ahead_copy = keep(remote(vsend.at[6], vrecv.at[6], v_s.at[6], v_r.at[6], zdev(1)))
    v_in[1].wait_recv()
    vsend[7] = (back + vrecv[5].astype(f32)).astype(bf16)
    back_copy = keep(remote(vsend.at[7], vrecv.at[7], v_s.at[7], v_r.at[7], zdev(nz - 1)))

    local[3].wait()
    local[4].wait()
    pltpu.make_async_copy(nrecv, nrecv, one_r.at[4]).wait()
    tile = nsend[...] + jnp.sum(nrecv[...], axis=0)
    total = jnp.sum(jnp.sum(tile, axis=1, keepdims=True), axis=0, keepdims=True)
    factor = jnp.minimum(1.0, clip_bound / (jnp.sqrt(total) + 1e-06))

    def update(i, c):
        at = pl.ds(pl.multiple_of(i * 64, 64), 64)
        rows_new = gfull[pl.ds(i * 4, 4)].reshape(64, 128)
        for j in range(4):
            cols = slice(j * 128, (j + 1) * 128)
            clipped = gown[at, cols] * factor
            moment = 0.9 * fm[at, cols].astype(f32) + 0.1 * clipped
            square = 0.95 * sm[at, cols].astype(f32) + 0.05 * clipped * clipped
            wf = w[at, cols].astype(f32)
            inner = wf - inner_rate * (moment / (jnp.sqrt(square) + 1e-08) + decay_rate * wf)
            merged = blend * inner + (1.0 - blend) * rows_new
            nw[at, cols] = jnp.where(frag == j, merged, inner).astype(bf16)
        return c

    lax.fori_loop(0, 8, update, 0)
    nw_copy = pltpu.make_async_copy(nw, nw_hbm, loc.at[5])
    nw_copy.start()

    ahead_copy.wait_recv()
    back_copy.wait_recv()
    vout[...] = (vown[...] + vrecv[6].astype(f32) + vrecv[7].astype(f32)).astype(bf16)
    v_out = pltpu.make_async_copy(vout, val_hbm, loc.at[6])
    v_out.start()

    for c in copies:
        c.wait_send()
    pltpu.make_async_copy(wrecv, wrecv, one_s.at[1]).wait()
    pltpu.make_async_copy(grow, grow, one_s.at[2]).wait()
    pltpu.make_async_copy(nrecv, nrecv, one_s.at[4]).wait()
    nw_copy.wait()
    v_out.wait()


def hand_over(*refs):
    n = len(refs) // 2
    sems = refs[-1]
    copies = [pltpu.make_async_copy(refs[i], refs[n + i], sems.at[i]) for i in range(n)]
    for c in copies:
        c.start()
    for c in copies:
        c.wait()


def per_device(n_rep, n_fsdp, tokens, norm_gain, weights, first_moment, second_moment, upstream, global_params, outer_momentum, fragment):
    nz = n_fsdp // 2
    bf, f32 = jnp.bfloat16, jnp.float32
    vm, anywhere = pl.BlockSpec(memory_space=pltpu.VMEM), pl.BlockSpec(memory_space=pl.ANY)
    dma = pltpu.SemaphoreType.DMA
    out = pl.pallas_call(
        functools.partial(kernel, n_rep, nz),
        out_shape=(
            jax.ShapeDtypeStruct((512, 512), bf),
            jax.ShapeDtypeStruct((128, 512), bf),
            jax.ShapeDtypeStruct(global_params.shape, f32),
            jax.ShapeDtypeStruct(outer_momentum.shape, f32),
        ),
        in_specs=[anywhere, vm, anywhere, anywhere, anywhere, anywhere, vm, vm, pl.BlockSpec(memory_space=pltpu.SMEM)],
        out_specs=(anywhere, anywhere, vm, vm),
        scratch_shapes=[
            pltpu.VMEM((128, 8192), bf),
            pltpu.VMEM((14, 128, 512), bf),
            pltpu.VMEM((8, 128, 512), bf),
            pltpu.VMEM((8, 128, 512), bf),
            pltpu.VMEM((512, 512), bf),
            pltpu.VMEM((512, 512), bf),
            pltpu.VMEM((8, 128, 512), bf),
            pltpu.VMEM((512, 512), bf),
            pltpu.VMEM((512, 512), bf),
            pltpu.VMEM((512, 512), bf),
            pltpu.VMEM((512, 512), f32),
            pltpu.VMEM((512, 512), bf),
            pltpu.VMEM((512, 512), bf),
            pltpu.VMEM((8, 128, 512), bf),
            pltpu.VMEM((8, 128, 512), bf),
            pltpu.VMEM((128, 512), f32),
            pltpu.VMEM((128, 512), bf),
            pltpu.VMEM((128, 128), f32),
            pltpu.VMEM((n_rep, 16, 128), bf),
            pltpu.VMEM((n_rep - 1, 16, 128), bf),
            pltpu.VMEM((16, 128), f32),
            pltpu.VMEM((n_rep - 1, 16, 128), f32),
            pltpu.VMEM((n_rep, 16, 128), f32),
            pltpu.VMEM((8, 128), f32),
            pltpu.VMEM((n_fsdp - 1, 8, 128), f32),
            dma((7,)),
            dma((14,)),
            dma((14,)),
            dma((8,)),
            dma((8,)),
            dma((8,)),
            dma((8,)),
            dma((5,)),
            dma((5,)),
        ],
        compiler_params=pltpu.CompilerParams(collective_id=0, has_side_effects=True, vmem_limit_bytes=60 * 1024 * 1024),
        name="step",
    )(
        tokens[0],
        norm_gain.reshape(64, 128),
        weights[0],
        first_moment[0],
        second_moment[0],
        upstream[0],
        global_params,
        outer_momentum,
        fragment,
    )
    out = pl.pallas_call(
        hand_over,
        out_shape=tuple(jax.ShapeDtypeStruct(o.shape, o.dtype) for o in out),
        in_specs=[anywhere] * 4,
        out_specs=(anywhere,) * 4,
        scratch_shapes=[dma((4,))],
        compiler_params=pltpu.CompilerParams(vmem_limit_bytes=60 * 1024 * 1024),
        name="hand_over",
    )(*out)
    return (out[0][None], out[1][None], out[2], out[3])


def solution(mesh):
    placed = (
        P("rep", "fsdp", None),
        P(),
        P("rep", "fsdp", None),
        P("rep", "fsdp", None),
        P("rep", "fsdp", None),
        P("rep", "fsdp", None),
        P(None, "fsdp", "rep", None),
        P(None, "fsdp", "rep", None),
        P(),
    )
    return jax.shard_map(
        functools.partial(per_device, mesh.shape["rep"], mesh.shape["fsdp"]),
        mesh=mesh,
        in_specs=placed,
        out_specs=(
            P("rep", "fsdp", None),
            P("rep", "fsdp", None),
            P(None, "fsdp", "rep", None),
            P(None, "fsdp", "rep", None),
        ),
        check_vma=False,
    )
```

time: 123 us -> 116 us (0.943)
  local copies, waits for them, and re-layouts: 6.18 us -> 0 us
    pallas_call x1, Pallas kernels: 115 us -> 91.3 us  [per_device(): pl.pallas_call(functools.partial(kernel, n_rep, nz), out_shape=(jax.Shape...]
    pallas_call x0 -> x1, Pallas kernels: none -> 23 us  [per_device(): pl.pallas_call(hand_over, out_shape=tuple((jax.ShapeDtypeStruct(o.shape,...]
    unnamed x4 -> x0, local copies, waits for them, and re-layouts: 6.18 us -> none
where the time goes in v2:
time: 116 us
  Pallas kernels  114 us (98%)
  between operations  1.29 us (1%)
    pallas_call x1, Pallas kernels, per_device(): pl.pallas_call(functools.partial(kernel, n_rep, nz), out_shape=(jax.Shape...  91.3 us
    pallas_call x1, Pallas kernels, per_device(): pl.pallas_call(hand_over, out_shape=tuple((jax.ShapeDtypeStruct(o.shape,...  23 us

profile of v2, /device:TPU:1, one launch (start us, length us, event | category | flops | bytes accessed | tf_op | source)
XLA Modules:
  0.0 115.6 jit_solution(12311359115963158227)
XLA Ops:
  1.3 91.3 %step.1 = (bf16[512,512]{1,0:T(8,128)(2,1)}, bf16[128,512]{1,0:T(8,128)(2,1)}, f32[4,1,16,128]{3,2,1,0:T(8,128)}, f32[4,1,16,128]{3,2,1,0:T(8,128)}) custom-call(bf16[128,8192]{1,0:T(8,128)(2,1)} %bitcast.8, f32[64,128]{1,0:T(8,128)} %bitcast.13, bf16[512,512]{1,0:T(8,128)(2,1)} %bitcast.9, bf16[512,512]{1,0:T(8,128)(2,1)} %bitcast.10, ...), custom_call_target="tpu_custom_call" | custom-call | tf_op jit(solution)/shard_map/step/pallas_call | solution.py:374
  92.6 23.0 %hand_over.1 = (bf16[512,512]{1,0:T(8,128)(2,1)}, bf16[128,512]{1,0:T(8,128)(2,1)}, f32[4,1,16,128]{3,2,1,0:T(8,128)}, f32[4,1,16,128]{3,2,1,0:T(8,128)}) custom-call(bf16[512,512]{1,0:T(8,128)(2,1)} %get-tuple-element.12.refs_0_, bf16[128,512]{1,0:T(8,128)(2,1)} %get-tuple-element.13.refs_1_, f32[4,1,16,128]{3,2,1,0:T(8,128)} %get-tuple-element.14.refs_2_, ...), custom_call_target="tpu_custom_call" | custom-call | tf_op jit(solution)/shard_map/hand_over/pallas_call | solution.py:433

commit v3 on v2

--- a/solution.py
+++ b/solution.py
@@ -25,16 +25,16 @@
     n_rep,
     nz,
     tok_hbm,
-    gain_ref,
+    gain_hbm,
     w_hbm,
     fm_hbm,
     sm_hbm,
     u_hbm,
-    gp_ref,
-    mom_ref,
+    gp_hbm,
+    mom_hbm,
     frag_ref,
-    nw_hbm,
-    val_hbm,
+    nw,
+    val,
     ng_ref,
     nm_ref,
     x,
@@ -46,14 +46,15 @@
     u,
     fm,
     sm,
-    nw,
+    gain_ref,
+    gp_ref,
+    mom_ref,
     gown,
     gsend,
     grecv,
     vsend,
     vrecv,
     vown,
-    vout,
     scale_ref,
     wsel,
     wrecv,
@@ -100,63 +101,31 @@
         return c
 
     local = [
-        pltpu.make_async_copy(tok_hbm, x, loc.at[0]),
-        pltpu.make_async_copy(w_hbm, w, loc.at[1]),
-        pltpu.make_async_copy(u_hbm, u.at[0], loc.at[2]),
-        pltpu.make_async_copy(fm_hbm, fm, loc.at[3]),
-        pltpu.make_async_copy(sm_hbm, sm, loc.at[4]),
+        pltpu.make_async_copy(src, dst, loc.at[n])
+        for n, (src, dst) in enumerate(
+            (
+                (u_hbm, u.at[0]),
+                (w_hbm, w),
+                (tok_hbm, x),
+                (gain_hbm, gain_ref),
+                (gp_hbm, gp_ref),
+                (mom_hbm, mom_ref),
+                (fm_hbm, fm),
+                (sm_hbm, sm),
+            )
+        )
     ]
     for c in local:
         c.start()
     lax.fori_loop(1, n_f, greet_f, 0)
     lax.fori_loop(1, n_rep, greet_r, 0)
 
-    frag = frag_ref[0]
-    local[0].wait()
-
-    def squares(i, acc):
-        for j in range(4):
-            v = x[:, pl.ds(pl.multiple_of(i * 512 + j * 128, 128), 128)].astype(f32)
-            acc = acc + v * v
-        return acc
-
-    acc = lax.fori_loop(0, 2 * nz, squares, jnp.zeros((rows, 128), f32))
-    mean = jnp.sum(acc, axis=1, keepdims=True) / (2 * nz * feats)
-    scale_ref[...] = jnp.broadcast_to(lax.rsqrt(mean + 1e-05), (rows, 128))
-
-    def normed(block, dst):
-        for j in range(4):
-            g = gain_ref[pl.ds(block * 4 + j, 1), :]
-            v = x[:, pl.ds(pl.multiple_of(block * feats + j * 128, 128), 128)].astype(f32)
-            dst[:, j * 128 : (j + 1) * 128] = (v * scale_ref[...] * g).astype(bf16)
-
     copies = []
 
     def keep(c):
         c.start()
         copies.append(c)
         return c
-
-    t_in = {}
-
-    def prepare(kind, i):
-        block = (1 - y if kind == 0 else y) * nz + (z + ORDER[i - 1]) % nz
-        normed(block, xn.at[kind * 7 + i - 1])
-
-    def send_tokens(kind, i):
-        n = kind * 7 + i - 1
-        t_in[kind, i] = keep(remote(xn.at[n], (to if kind else tp).at[i], t_s.at[n], t_r.at[n], zdev(ORDER[i - 1])))
-
-    for i in FAR[:3]:
-        prepare(0, i)
-    local[1].wait()
-    sel = w[:, 0:128]
-    for j in range(1, 4):
-        sel = jnp.where(frag == j, w[:, j * 128 : (j + 1) * 128], sel)
-    wsel[...] = sel.reshape(wsel.shape)
-    local[2].wait()
-
-    pl.semaphore_wait(barrier, n_f - 1 + n_rep - 1)
 
     def hop(h):
         part = [slice(0, rows), slice(0, rows)] if h < 4 else [slice(0, rows // 2), slice(rows // 2, rows)]
@@ -165,10 +134,48 @@
             for n, (s, p) in enumerate(zip((AHEAD, BACK), part))
         ]
 
+    local[0].wait()
+    pl.semaphore_wait(barrier, n_f - 1 + n_rep - 1)
     u_in = hop(1)
+    local[1].wait()
+    w_copy = keep(remote(w, wp, one_s.at[0], one_r.at[0], partner))
+    local[2].wait()
+
+    def squares(i, acc):
+        for j in range(4):
+            v = x[:, pl.ds(pl.multiple_of(i * 512 + j * 128, 128), 128)].astype(f32)
+            acc = acc + v * v
+        return acc
+
+    acc = lax.fori_loop(0, 2 * nz, squares, jnp.zeros((rows, 128), f32))
+    mean = jnp.sum(acc, axis=1, keepdims=True) / (2 * nz * feats)
+    scale_ref[...] = jnp.broadcast_to(lax.rsqrt(mean + 1e-05), (rows, 128))
+
+    def normed(block, dst):
+        for j in range(4):
+            g = gain_ref[pl.ds(block * 4 + j, 1), :]
+            v = x[:, pl.ds(pl.multiple_of(block * feats + j * 128, 128), 128)].astype(f32)
+            dst[:, j * 128 : (j + 1) * 128] = (v * scale_ref[...] * g).astype(bf16)
+
+    t_in = {}
+
+    def prepare(kind, i):
+        block = (1 - y if kind == 0 else y) * nz + (z + ORDER[i - 1]) % nz
+        normed(block, xn.at[kind * 7 + i - 1])
+
+    def send_tokens(kind, i):
+        n = kind * 7 + i - 1
+        t_in[kind, i] = keep(remote(xn.at[n], (to if kind else tp).at[i], t_s.at[n], t_r.at[n], zdev(ORDER[i - 1])))
+
+    local[3].wait()
     for i in FAR[:3]:
+        prepare(0, i)
         send_tokens(0, i)
-    w_copy = keep(remote(w, wp, one_s.at[0], one_r.at[0], partner))
+    frag = frag_ref[0]
+    sel = w[:, 0:128]
+    for j in range(1, 4):
+        sel = jnp.where(frag == j, w[:, j * 128 : (j + 1) * 128], sel)
+    wsel[...] = sel.reshape(wsel.shape)
 
     def send_rows(k, c):
         dst = (r + k) % n_rep
@@ -200,6 +207,8 @@
         return acc + wrecv[k].astype(f32)
 
     total_rows = lax.fori_loop(0, n_rep - 1, add_rows, wsel[r].astype(f32))
+    local[4].wait()
+    local[5].wait()
     share_g, share_u = gp_ref[0, 0], mom_ref[0, 0]
     for j in range(1, 4):
         share_g = jnp.where(frag == j, gp_ref[j, 0], share_g)
@@ -267,30 +276,32 @@
 
     lax.fori_loop(1, n_rep, place, 0)
 
-    for s in (2, 3):
-        a, b = {2: (6, 5), 3: (4, 3)}[s]
-        at = 2 * s - 2
-        t_in[1, a].wait_recv()
-        ahead = partial(a)
-        t_in[1, b].wait_recv()
-        back = partial(b)
-        v_in[0].wait_recv()
-        if s == 2:
-            vsend[at, first_half] = (ahead[first_half] + vrecv[0, first_half].astype(f32)).astype(bf16)
-            vsend[at, last_half] = ahead[last_half].astype(bf16)
-        else:
-            vsend[at] = (ahead + vrecv[at - 2].astype(f32)).astype(bf16)
-        ahead_copy = keep(remote(vsend.at[at], vrecv.at[at], v_s.at[at], v_r.at[at], zdev(1)))
-        v_in[1].wait_recv()
-        if s == 2:
-            vsend[at + 1, last_half] = (back[last_half] + vrecv[0, last_half].astype(f32)).astype(bf16)
-            vsend[at + 1, first_half] = back[first_half].astype(bf16)
-        else:
-            vsend[at + 1] = (back + vrecv[at - 1].astype(f32)).astype(bf16)
-        back_copy = keep(remote(vsend.at[at + 1], vrecv.at[at + 1], v_s.at[at + 1], v_r.at[at + 1], zdev(nz - 1)))
-        v_in = [ahead_copy, back_copy]
-        for m in halves:
-            gown[m, :] += grad(to, b, 2, m)
+    def ring(at, ahead, back):
+        out = []
+        for n, part in enumerate((ahead, back)):
+            v_in[n].wait_recv()
+            if at == 2:
+                mine, other = (first_half, last_half)[n], (last_half, first_half)[n]
+                vsend[at + n, mine] = (part[mine] + vrecv[0, mine].astype(f32)).astype(bf16)
+                vsend[at + n, other] = part[other].astype(bf16)
+            else:
+                vsend[at + n] = (part + vrecv[at - 2 + n].astype(f32)).astype(bf16)
+            out.append(
+                keep(remote(vsend.at[at + n], vrecv.at[at + n], v_s.at[at + n], v_r.at[at + n], zdev((1, nz - 1)[n])))
+            )
+        return out
+
+    t_in[1, 6].wait_recv()
+    t_in[1, 5].wait_recv()
+    v_in = ring(2, partial(6), partial(5))
+    for m in halves:
+        gown[m, :] += grad(to, 5, 2, m)
+
+    t_in[1, 4].wait_recv()
+    t_in[1, 3].wait_recv()
+    v_in = ring(4, partial(4), partial(3))
+    for m in halves:
+        gown[m, :] += grad(to, 3, 2, m)
 
     g_copy.wait_recv()
     t_in[1, 1].wait_recv()
@@ -308,16 +319,10 @@
 
     lax.fori_loop(1, n_f, send_norm, 0)
 
-    ahead, back = partial(2), partial(1)
-    v_in[0].wait_recv()
-    vsend[6] = (ahead + vrecv[4].astype(f32)).astype(bf16)
-    ahead_copy = keep(remote(vsend.at[6], vrecv.at[6], v_s.at[6], v_r.at[6], zdev(1)))
-    v_in[1].wait_recv()
-    vsend[7] = (back + vrecv[5].astype(f32)).astype(bf16)
-    back_copy = keep(remote(vsend.at[7], vrecv.at[7], v_s.at[7], v_r.at[7], zdev(nz - 1)))
-
-    local[3].wait()
-    local[4].wait()
+    ahead_copy, back_copy = ring(6, partial(2), partial(1))
+
+    local[6].wait()
+    local[7].wait()
     pltpu.make_async_copy(nrecv, nrecv, one_r.at[4]).wait()
     tile = nsend[...] + jnp.sum(nrecv[...], axis=0)
     total = jnp.sum(jnp.sum(tile, axis=1, keepdims=True), axis=0, keepdims=True)
@@ -338,22 +343,16 @@
         return c
 
     lax.fori_loop(0, 8, update, 0)
-    nw_copy = pltpu.make_async_copy(nw, nw_hbm, loc.at[5])
-    nw_copy.start()
 
     ahead_copy.wait_recv()
     back_copy.wait_recv()
-    vout[...] = (vown[...] + vrecv[6].astype(f32) + vrecv[7].astype(f32)).astype(bf16)
-    v_out = pltpu.make_async_copy(vout, val_hbm, loc.at[6])
-    v_out.start()
+    val[...] = (vown[...] + vrecv[6].astype(f32) + vrecv[7].astype(f32)).astype(bf16)
 
     for c in copies:
         c.wait_send()
     pltpu.make_async_copy(wrecv, wrecv, one_s.at[1]).wait()
     pltpu.make_async_copy(grow, grow, one_s.at[2]).wait()
     pltpu.make_async_copy(nrecv, nrecv, one_s.at[4]).wait()
-    nw_copy.wait()
-    v_out.wait()
 
 
 def hand_over(*refs):
@@ -374,13 +373,13 @@
     out = pl.pallas_call(
         functools.partial(kernel, n_rep, nz),
         out_shape=(
-            jax.ShapeDtypeStruct((512, 512), bf),
-            jax.ShapeDtypeStruct((128, 512), bf),
-            jax.ShapeDtypeStruct(global_params.shape, f32),
-            jax.ShapeDtypeStruct(outer_momentum.shape, f32),
+            pltpu.VMEM((512, 512), bf),
+            pltpu.VMEM((128, 512), bf),
+            pltpu.VMEM(global_params.shape, f32),
+            pltpu.VMEM(outer_momentum.shape, f32),
         ),
-        in_specs=[anywhere, vm, anywhere, anywhere, anywhere, anywhere, vm, vm, pl.BlockSpec(memory_space=pltpu.SMEM)],
-        out_specs=(anywhere, anywhere, vm, vm),
+        in_specs=[anywhere] * 8 + [pl.BlockSpec(memory_space=pltpu.SMEM)],
+        out_specs=(vm,) * 4,
         scratch_shapes=[
             pltpu.VMEM((128, 8192), bf),
             pltpu.VMEM((14, 128, 512), bf),
@@ -391,14 +390,15 @@
             pltpu.VMEM((8, 128, 512), bf),
             pltpu.VMEM((512, 512), bf),
             pltpu.VMEM((512, 512), bf),
-            pltpu.VMEM((512, 512), bf),
+            pltpu.VMEM((64, 128), f32),
+            pltpu.VMEM(global_params.shape, f32),
+            pltpu.VMEM(outer_momentum.shape, f32),
             pltpu.VMEM((512, 512), f32),
             pltpu.VMEM((512, 512), bf),
             pltpu.VMEM((512, 512), bf),
             pltpu.VMEM((8, 128, 512), bf),
             pltpu.VMEM((8, 128, 512), bf),
             pltpu.VMEM((128, 512), f32),
-            pltpu.VMEM((128, 512), bf),
             pltpu.VMEM((128, 128), f32),
             pltpu.VMEM((n_rep, 16, 128), bf),
             pltpu.VMEM((n_rep - 1, 16, 128), bf),
@@ -407,7 +407,7 @@
             pltpu.VMEM((n_rep, 16, 128), f32),
             pltpu.VMEM((8, 128), f32),
             pltpu.VMEM((n_fsdp - 1, 8, 128), f32),
-            dma((7,)),
+            dma((8,)),
             dma((14,)),
             dma((14,)),
             dma((8,)),
@@ -417,28 +417,32 @@
             dma((5,)),
             dma((5,)),
         ],
-        compiler_params=pltpu.CompilerParams(collective_id=0, has_side_effects=True, vmem_limit_bytes=60 * 1024 * 1024),
+        compiler_params=pltpu.CompilerParams(collective_id=0, has_side_effects=True, vmem_limit_bytes=40 * 1024 * 1024),
         name="step",
     )(
-        tokens[0],
-        norm_gain.reshape(64, 128),
-        weights[0],
-        first_moment[0],
-        second_moment[0],
-        upstream[0],
-        global_params,
-        outer_momentum,
+        *(
+            pltpu.with_memory_space_constraint(a, pltpu.HBM)
+            for a in (
+                tokens[0],
+                norm_gain.reshape(64, 128),
+                weights[0],
+                first_moment[0],
+                second_moment[0],
+                upstream[0],
+                global_params,
+                outer_momentum,
+            )
+        ),
         fragment,
     )
     out = pl.pallas_call(
         hand_over,
-        out_shape=tuple(jax.ShapeDtypeStruct(o.shape, o.dtype) for o in out),
-        in_specs=[anywhere] * 4,
+        out_shape=tuple(pltpu.HBM(o.shape, o.dtype) for o in out),
+        in_specs=[vm] * 4,
         out_specs=(anywhere,) * 4,
         scratch_shapes=[dma((4,))],
-        compiler_params=pltpu.CompilerParams(vmem_limit_bytes=60 * 1024 * 1024),
         name="hand_over",
-    )(*out)
+    )(*(pltpu.with_memory_space_constraint(o, pltpu.VMEM) for o in out))
     return (out[0][None], out[1][None], out[2], out[3])
 
 

time: 116 us -> 92.3 us (0.80)
  Pallas kernels: 114 us -> 90.3 us
    pallas_call x2, Pallas kernels: 114 us -> 90.3 us  [the longest x1 89.5 us: per_device(): pl.pallas_call(functools.partial(kernel, n_rep, nz), out_shape=(pltpu.VME...]
where the time goes in v3:
time: 92.3 us; the launch traced here: 91.6 us
  Pallas kernels  90.3 us (98%)
  between operations  1.29 us (1%)
    pallas_call x1, Pallas kernels, per_device(): pl.pallas_call(functools.partial(kernel, n_rep, nz), out_shape=(pltpu.VME...  89.5 us

profile of v3, /device:TPU:1, one launch (start us, length us, event | category | flops | bytes accessed | tf_op | source)
XLA Modules:
  0.0 91.6 jit_solution(8628825017929246296)
XLA Ops:
  1.3 89.5 %step.1 = (bf16[512,512]{1,0:T(8,128)(2,1)S(1)}, bf16[128,512]{1,0:T(8,128)(2,1)S(1)}, f32[4,1,16,128]{3,2,1,0:T(8,128)S(1)}, f32[4,1,16,128]{3,2,1,0:T(8,128)S(1)}) custom-call(bf16[128,8192]{1,0:T(8,128)(2,1)} %bitcast.8, f32[64,128]{1,0:T(8,128)} %bitcast.13, bf16[512,512]{1,0:T(8,128)(2,1)} %bitcast.9, bf16[512,512]{1,0:T(8,128)(2,1)} %bitcast.10, ...), custom_call_target="tpu_custom_call" | custom-call | tf_op jit(solution)/shard_map/step/pallas_call | solution.py:373
  90.8 0.9 hand_over.1

commit v4 on v3

--- a/solution.py
+++ b/solution.py
@@ -18,7 +18,6 @@
 
 ORDER = (1, 7, 2, 6, 3, 5, 4)
 AHEAD, BACK = (0, 1, 3, 5, 7), (0, 2, 4, 6, 7)
-FAR = (7, 5, 6, 3, 4, 1, 2)
 
 
 def kernel(
@@ -72,6 +71,7 @@
     v_r,
     one_s,
     one_r,
+    hello,
 ):
     r = lax.axis_index("rep")
     f = lax.axis_index("fsdp")
@@ -96,8 +96,18 @@
         pl.semaphore_signal(barrier, inc=1, device_id={"rep": r, "fsdp": (f + k) % n_f}, device_id_type=MESH)
         return c
 
-    def greet_r(k, c):
-        pl.semaphore_signal(barrier, inc=1, device_id={"rep": (r + k) % n_rep, "fsdp": f}, device_id_type=MESH)
+    half = n_rep // 2
+    rank = (r % 2) * half + r // 2
+
+    def at_rank(q):
+        return {"rep": (q % half) * 2 + q // half, "fsdp": f}
+
+    def greet_r(q, c):
+        pl.semaphore_signal(barrier, inc=1, device_id=at_rank(q), device_id_type=MESH)
+        return c
+
+    def say_hello(q, c):
+        pl.semaphore_signal(hello, inc=1, device_id=at_rank(q), device_id_type=MESH)
         return c
 
     local = [
@@ -118,7 +128,7 @@
     for c in local:
         c.start()
     lax.fori_loop(1, n_f, greet_f, 0)
-    lax.fori_loop(1, n_rep, greet_r, 0)
+    lax.fori_loop(rank + 1, n_rep, greet_r, 0)
 
     copies = []
 
@@ -135,7 +145,7 @@
         ]
 
     local[0].wait()
-    pl.semaphore_wait(barrier, n_f - 1 + n_rep - 1)
+    pl.semaphore_wait(barrier, n_f - 1 + rank)
     u_in = hop(1)
     local[1].wait()
     w_copy = keep(remote(w, wp, one_s.at[0], one_r.at[0], partner))
@@ -167,70 +177,14 @@
         n = kind * 7 + i - 1
         t_in[kind, i] = keep(remote(xn.at[n], (to if kind else tp).at[i], t_s.at[n], t_r.at[n], zdev(ORDER[i - 1])))
 
-    local[3].wait()
-    for i in FAR[:3]:
-        prepare(0, i)
-        send_tokens(0, i)
-    frag = frag_ref[0]
-    sel = w[:, 0:128]
-    for j in range(1, 4):
-        sel = jnp.where(frag == j, w[:, j * 128 : (j + 1) * 128], sel)
-    wsel[...] = sel.reshape(wsel.shape)
-
     def send_rows(k, c):
         dst = (r + k) % n_rep
         remote(wsel.at[dst], wrecv.at[k - 1], one_s.at[1], one_r.at[1], {"rep": dst, "fsdp": f}).start()
         return c
 
-    lax.fori_loop(1, n_rep, send_rows, 0)
-    for i in FAR[3:]:
-        prepare(0, i)
-
-    for c in u_in:
-        c.wait_recv()
-    u_in = hop(2)
-    for i in FAR[3:5]:
-        send_tokens(0, i)
-    normed((1 - y) * nz + z, tp.at[0])
-    normed(y * nz + z, to.at[0])
-    for c in u_in:
-        c.wait_recv()
-    u_in = hop(3)
-    for i in FAR[5:]:
-        send_tokens(0, i)
-    for i in FAR:
-        prepare(1, i)
-
-    pltpu.make_async_copy(wrecv, wrecv, one_r.at[1]).wait()
-
-    def add_rows(k, acc):
-        return acc + wrecv[k].astype(f32)
-
-    total_rows = lax.fori_loop(0, n_rep - 1, add_rows, wsel[r].astype(f32))
-    local[4].wait()
-    local[5].wait()
-    share_g, share_u = gp_ref[0, 0], mom_ref[0, 0]
-    for j in range(1, 4):
-        share_g = jnp.where(frag == j, gp_ref[j, 0], share_g)
-        share_u = jnp.where(frag == j, mom_ref[j, 0], share_u)
-    delta = share_g - total_rows / n_rep
-    u_new = outer_mom * share_u + delta
-    g_new = share_g - outer_rate * (outer_mom * u_new + delta)
-    gnew[...] = g_new
-
-    def send_new(k, c):
-        remote(gnew, grow.at[k - 1], one_s.at[2], one_r.at[2], {"rep": (r + k) % n_rep, "fsdp": f}).start()
-        return c
-
-    for c in u_in:
-        c.wait_recv()
-    u_in = hop(4)
-    for i in FAR:
-        send_tokens(1, i)
-    lax.fori_loop(1, n_rep, send_new, 0)
-    for j in range(4):
-        ng_ref[j, 0] = jnp.where(frag == j, g_new, gp_ref[j, 0])
-        nm_ref[j, 0] = jnp.where(frag == j, u_new, mom_ref[j, 0])
+    def wait_all(cs):
+        for c in cs:
+            c.wait_recv()
 
     def grad(t, first, count, cols):
         k = count * rows
@@ -241,40 +195,16 @@
             preferred_element_type=f32,
         )
 
-    for i in FAR:
-        t_in[0, i].wait_recv()
-    for c in u_in:
-        c.wait_recv()
-    halves = (slice(0, 256), slice(256, 512))
-    for m in halves:
-        gsend[m, :] = grad(tp, 0, nz, m).astype(bf16)
-    g_copy = keep(remote(gsend, grecv, one_s.at[3], one_r.at[3], partner))
-
-    w_copy.wait_recv()
-
     def partial(i):
         return jnp.dot(tp[i], wp[...], preferred_element_type=f32) + jnp.dot(to[i], w[...], preferred_element_type=f32)
 
-    vown[...] = partial(0)
-
-    t_in[1, 7].wait_recv()
-    vsend[0] = partial(7).astype(bf16)
+    def wait_tokens(*slots):
+        for i in slots:
+            t_in[0, i].wait_recv()
+            t_in[1, i].wait_recv()
+
+    halves = (slice(0, 256), slice(256, 512))
     first_half, last_half = slice(0, rows // 2), slice(rows // 2, rows)
-    v_in = [
-        keep(remote(vsend.at[0, p], vrecv.at[0, p], v_s.at[n], v_r.at[n], zdev((1, nz - 1)[n])))
-        for n, p in enumerate((first_half, last_half))
-    ]
-    for m in halves:
-        gown[m, :] = grad(to, 0, 1, m) + grad(to, 7, 1, m)
-
-    pltpu.make_async_copy(grow, grow, one_r.at[2]).wait()
-    gfull[r] = gnew[...]
-
-    def place(k, c):
-        gfull[(r + n_rep - k) % n_rep] = grow[k - 1]
-        return c
-
-    lax.fori_loop(1, n_rep, place, 0)
 
     def ring(at, ahead, back):
         out = []
@@ -291,21 +221,103 @@
             )
         return out
 
+    local[3].wait()
+    for i in (7, 5, 6):
+        prepare(0, i)
+        send_tokens(0, i)
+    frag = frag_ref[0]
+    sel = w[:, 0:128]
+    for j in range(1, 4):
+        sel = jnp.where(frag == j, w[:, j * 128 : (j + 1) * 128], sel)
+    wsel[...] = sel.reshape(wsel.shape)
+    lax.fori_loop(0, rank, say_hello, 0)
+    for i in (3, 4, 1, 2):
+        prepare(0, i)
+
+    wait_all(u_in)
+    u_in = hop(2)
+    send_tokens(0, 3)
+    send_tokens(0, 4)
+    normed((1 - y) * nz + z, tp.at[0])
+    normed(y * nz + z, to.at[0])
+    for i in (7, 5, 6):
+        prepare(1, i)
+    wait_all(u_in)
+    u_in = hop(3)
+    send_tokens(0, 1)
+    send_tokens(0, 2)
+
+    @pl.when(rank < n_rep - 1)
+    def _():
+        pl.semaphore_wait(hello, n_rep - 1 - rank)
+
+    lax.fori_loop(1, n_rep, send_rows, 0)
+    for i in (3, 4, 1, 2):
+        prepare(1, i)
+    w_copy.wait_recv()
+    vown[...] = partial(0)
+    wait_all(u_in)
+    u_in = hop(4)
+    send_tokens(1, 7)
+    send_tokens(1, 5)
+    send_tokens(1, 6)
+    for i in (7, 5, 6, 3, 4, 1, 2):
+        t_in[0, i].wait_recv()
+    wait_all(u_in)
+    for m in halves:
+        gsend[m, :] = grad(tp, 0, nz, m).astype(bf16)
+    g_copy = keep(remote(gsend, grecv, one_s.at[3], one_r.at[3], partner))
+    t_in[1, 7].wait_recv()
+    vsend[0] = partial(7).astype(bf16)
+    v_in = [
+        keep(remote(vsend.at[0, p], vrecv.at[0, p], v_s.at[n], v_r.at[n], zdev((1, nz - 1)[n])))
+        for n, p in enumerate((first_half, last_half))
+    ]
+    send_tokens(1, 3)
+    send_tokens(1, 4)
+    for m in halves:
+        gown[m, :] = grad(to, 0, 1, m) + grad(to, 7, 1, m)
+    pltpu.make_async_copy(wrecv, wrecv, one_r.at[1]).wait()
+
+    def add_rows(k, acc):
+        return acc + wrecv[k].astype(f32)
+
+    total_rows = lax.fori_loop(0, n_rep - 1, add_rows, wsel[r].astype(f32))
+    local[4].wait()
+    local[5].wait()
+    share_g, share_u = gp_ref[0, 0], mom_ref[0, 0]
+    for j in range(1, 4):
+        share_g = jnp.where(frag == j, gp_ref[j, 0], share_g)
+        share_u = jnp.where(frag == j, mom_ref[j, 0], share_u)
+    delta = share_g - total_rows / n_rep
+    u_new = outer_mom * share_u + delta
+    g_new = share_g - outer_rate * (outer_mom * u_new + delta)
+    gnew[...] = g_new
+
+    def send_new(k, c):
+        remote(gnew, grow.at[k - 1], one_s.at[2], one_r.at[2], {"rep": (r + k) % n_rep, "fsdp": f}).start()
+        return c
+
+    lax.fori_loop(1, n_rep, send_new, 0)
+    for j in range(4):
+        ng_ref[j, 0] = jnp.where(frag == j, g_new, gp_ref[j, 0])
+        nm_ref[j, 0] = jnp.where(frag == j, u_new, mom_ref[j, 0])
+
     t_in[1, 6].wait_recv()
     t_in[1, 5].wait_recv()
     v_in = ring(2, partial(6), partial(5))
+    send_tokens(1, 1)
+    send_tokens(1, 2)
     for m in halves:
         gown[m, :] += grad(to, 5, 2, m)
-
     t_in[1, 4].wait_recv()
     t_in[1, 3].wait_recv()
     v_in = ring(4, partial(4), partial(3))
     for m in halves:
         gown[m, :] += grad(to, 3, 2, m)
-
-    g_copy.wait_recv()
     t_in[1, 1].wait_recv()
     t_in[1, 2].wait_recv()
+    g_copy.wait_recv()
     acc = jnp.zeros((8, feats), f32)
     for m in halves:
         g = gown[m, :] + grecv[m, :].astype(f32) + grad(to, 1, 2, m)
@@ -319,7 +331,15 @@
 
     lax.fori_loop(1, n_f, send_norm, 0)
 
-    ahead_copy, back_copy = ring(6, partial(2), partial(1))
+    v_in = ring(6, partial(2), partial(1))
+    pltpu.make_async_copy(grow, grow, one_r.at[2]).wait()
+    gfull[r] = gnew[...]
+
+    def place(k, c):
+        gfull[(r + n_rep - k) % n_rep] = grow[k - 1]
+        return c
+
+    lax.fori_loop(1, n_rep, place, 0)
 
     local[6].wait()
     local[7].wait()
@@ -344,8 +364,7 @@
 
     lax.fori_loop(0, 8, update, 0)
 
-    ahead_copy.wait_recv()
-    back_copy.wait_recv()
+    wait_all(v_in)
     val[...] = (vown[...] + vrecv[6].astype(f32) + vrecv[7].astype(f32)).astype(bf16)
 
     for c in copies:
@@ -416,6 +435,7 @@
             dma((8,)),
             dma((5,)),
             dma((5,)),
+            pltpu.SemaphoreType.REGULAR,
         ],
         compiler_params=pltpu.CompilerParams(collective_id=0, has_side_effects=True, vmem_limit_bytes=40 * 1024 * 1024),
         name="step",

time: 92.3 us -> 87.5 us (0.948)
  the two profiles are of different devices: /device:TPU:1 before, /device:TPU:6 now
where the time goes in v4:
time: 87.5 us; the launch traced here: 87.4 us
  Pallas kernels  86.1 us (98%)
  between operations  1.29 us (1%)
    pallas_call x1, Pallas kernels, per_device(): pl.pallas_call(functools.partial(kernel, n_rep, nz), out_shape=(pltpu.VME...  85.3 us

profile of v4, /device:TPU:6, one launch (start us, length us, event | category | flops | bytes accessed | tf_op | source)
XLA Modules:
  0.0 87.4 jit_solution(9273558603493547272)
XLA Ops:
  1.3 85.3 %step.1 = (bf16[512,512]{1,0:T(8,128)(2,1)S(1)}, bf16[128,512]{1,0:T(8,128)(2,1)S(1)}, f32[4,1,16,128]{3,2,1,0:T(8,128)S(1)}, f32[4,1,16,128]{3,2,1,0:T(8,128)S(1)}) custom-call(bf16[128,8192]{1,0:T(8,128)(2,1)} %bitcast.8, f32[64,128]{1,0:T(8,128)} %bitcast.13, bf16[512,512]{1,0:T(8,128)(2,1)} %bitcast.9, bf16[512,512]{1,0:T(8,128)(2,1)} %bitcast.10, ...), custom_call_target="tpu_custom_call" | custom-call | tf_op jit(solution)/shard_map/step/pallas_call | solution.py:392
  86.5 0.9 %hand_over.1 = (bf16[512,512]{1,0:T(8,128)(2,1)}, bf16[128,512]{1,0:T(8,128)(2,1)}, f32[4,1,16,128]{3,2,1,0:T(8,128)}, f32[4,1,16,128]{3,2,1,0:T(8,128)}) custom-call(bf16[512,512]{1,0:T(8,128)(2,1)S(1)} %get-tuple-element.12.refs_0_, bf16[128,512]{1,0:T(8,128)(2,1)S(1)} %get-tuple-element.13.refs_1_, f32[4,1,16,128]{3,2,1,0:T(8,128)S(1)} %get-tuple-element.14.refs_2_, ...), custom_call_target="tpu_custom_call" | custom-call | tf_op jit(solution)/shard_map/hand_over/pallas_call | solution.py:458

commit v5 on v4

--- a/solution.py
+++ b/solution.py
@@ -96,11 +96,11 @@
         pl.semaphore_signal(barrier, inc=1, device_id={"rep": r, "fsdp": (f + k) % n_f}, device_id_type=MESH)
         return c
 
-    half = n_rep // 2
-    rank = (r % 2) * half + r // 2
+    half, quad = n_rep // 2, n_rep // 8
+    rank = (r % 2) * half + (r // 2 % 4) * quad + r // 8
 
     def at_rank(q):
-        return {"rep": (q % half) * 2 + q // half, "fsdp": f}
+        return {"rep": (q % quad) * 8 + (q % half) // quad * 2 + q // half, "fsdp": f}
 
     def greet_r(q, c):
         pl.semaphore_signal(barrier, inc=1, device_id=at_rank(q), device_id_type=MESH)
@@ -259,9 +259,11 @@
     wait_all(u_in)
     u_in = hop(4)
     send_tokens(1, 7)
+    for i in (7, 5, 6):
+        t_in[0, i].wait_recv()
     send_tokens(1, 5)
     send_tokens(1, 6)
-    for i in (7, 5, 6, 3, 4, 1, 2):
+    for i in (3, 4, 1, 2):
         t_in[0, i].wait_recv()
     wait_all(u_in)
     for m in halves:
@@ -273,10 +275,13 @@
         keep(remote(vsend.at[0, p], vrecv.at[0, p], v_s.at[n], v_r.at[n], zdev((1, nz - 1)[n])))
         for n, p in enumerate((first_half, last_half))
     ]
+    for m in halves:
+        gown[m, :] = grad(to, 0, 1, m) + grad(to, 7, 1, m)
     send_tokens(1, 3)
     send_tokens(1, 4)
-    for m in halves:
-        gown[m, :] = grad(to, 0, 1, m) + grad(to, 7, 1, m)
+    t_in[1, 6].wait_recv()
+    t_in[1, 5].wait_recv()
+    v_in = ring(2, partial(6), partial(5))
     pltpu.make_async_copy(wrecv, wrecv, one_r.at[1]).wait()
 
     def add_rows(k, acc):
@@ -303,15 +308,12 @@
         ng_ref[j, 0] = jnp.where(frag == j, g_new, gp_ref[j, 0])
         nm_ref[j, 0] = jnp.where(frag == j, u_new, mom_ref[j, 0])
 
-    t_in[1, 6].wait_recv()
-    t_in[1, 5].wait_recv()
-    v_in = ring(2, partial(6), partial(5))
-    send_tokens(1, 1)
-    send_tokens(1, 2)
     for m in halves:
         gown[m, :] += grad(to, 5, 2, m)
     t_in[1, 4].wait_recv()
     t_in[1, 3].wait_recv()
+    send_tokens(1, 1)
+    send_tokens(1, 2)
     v_in = ring(4, partial(4), partial(3))
     for m in halves:
         gown[m, :] += grad(to, 3, 2, m)

time: 87.5 us -> 86.2 us (0.985)
  the two profiles are of different devices: /device:TPU:6 before, /device:TPU:1 now
where the time goes in v5:
time: 86.2 us; the launch traced here: 85.5 us
  Pallas kernels  84.2 us (98%)
  between operations  1.29 us (1%)
    pallas_call x1, Pallas kernels, per_device(): pl.pallas_call(functools.partial(kernel, n_rep, nz), out_shape=(pltpu.VME...  83.3 us

profile of v5, /device:TPU:1, one launch (start us, length us, event | category | flops | bytes accessed | tf_op | source)
XLA Modules:
  0.0 85.5 jit_solution(2480763047950413110)
XLA Ops:
  1.3 83.3 %step.1 = (bf16[512,512]{1,0:T(8,128)(2,1)S(1)}, bf16[128,512]{1,0:T(8,128)(2,1)S(1)}, f32[4,1,16,128]{3,2,1,0:T(8,128)S(1)}, f32[4,1,16,128]{3,2,1,0:T(8,128)S(1)}) custom-call(bf16[128,8192]{1,0:T(8,128)(2,1)} %bitcast.8, f32[64,128]{1,0:T(8,128)} %bitcast.13, bf16[512,512]{1,0:T(8,128)(2,1)} %bitcast.9, bf16[512,512]{1,0:T(8,128)(2,1)} %bitcast.10, ...), custom_call_target="tpu_custom_call" | custom-call | tf_op jit(solution)/shard_map/step/pallas_call | solution.py:394
  84.6 0.9 %hand_over.1 = (bf16[512,512]{1,0:T(8,128)(2,1)}, bf16[128,512]{1,0:T(8,128)(2,1)}, f32[4,1,16,128]{3,2,1,0:T(8,128)}, f32[4,1,16,128]{3,2,1,0:T(8,128)}) custom-call(bf16[512,512]{1,0:T(8,128)(2,1)S(1)} %get-tuple-element.12.refs_0_, bf16[128,512]{1,0:T(8,128)(2,1)S(1)} %get-tuple-element.13.refs_1_, f32[4,1,16,128]{3,2,1,0:T(8,128)S(1)} %get-tuple-element.14.refs_2_, ...), custom_call_target="tpu_custom_call" | custom-call | tf_op jit(solution)/shard_map/hand_over/pallas_call | solution.py:460

commit v6 on v5

--- a/solution.py
+++ b/solution.py
@@ -125,10 +125,12 @@
             )
         )
     ]
-    for c in local:
+    lax.fori_loop(1, n_f, greet_f, 0)
+    for c in local[:3]:
         c.start()
-    lax.fori_loop(1, n_f, greet_f, 0)
     lax.fori_loop(rank + 1, n_rep, greet_r, 0)
+    for c in local[3:]:
+        c.start()
 
     copies = []
 

time: 86.2 us -> 86.3 us (level)
  no operation moved by 1% of the time
where the time goes in v6:
time: 86.3 us; the launch traced here: 85.7 us
  Pallas kernels  84.4 us (98%)
  between operations  1.29 us (1%)
    pallas_call x1, Pallas kernels, per_device(): pl.pallas_call(functools.partial(kernel, n_rep, nz), out_shape=(pltpu.VME...  83.5 us

profile of v6, /device:TPU:1, one launch (start us, length us, event | category | flops | bytes accessed | tf_op | source)
XLA Modules:
  0.0 85.7 jit_solution(16782761472000125514)
XLA Ops:
  1.3 83.5 %step.1 = (bf16[512,512]{1,0:T(8,128)(2,1)S(1)}, bf16[128,512]{1,0:T(8,128)(2,1)S(1)}, f32[4,1,16,128]{3,2,1,0:T(8,128)S(1)}, f32[4,1,16,128]{3,2,1,0:T(8,128)S(1)}) custom-call(bf16[128,8192]{1,0:T(8,128)(2,1)} %bitcast.8, f32[64,128]{1,0:T(8,128)} %bitcast.13, bf16[512,512]{1,0:T(8,128)(2,1)} %bitcast.9, bf16[512,512]{1,0:T(8,128)(2,1)} %bitcast.10, ...), custom_call_target="tpu_custom_call" | custom-call | tf_op jit(solution)/shard_map/step/pallas_call | solution.py:396
  84.8 0.9 %hand_over.1 = (bf16[512,512]{1,0:T(8,128)(2,1)}, bf16[128,512]{1,0:T(8,128)(2,1)}, f32[4,1,16,128]{3,2,1,0:T(8,128)}, f32[4,1,16,128]{3,2,1,0:T(8,128)}) custom-call(bf16[512,512]{1,0:T(8,128)(2,1)S(1)} %get-tuple-element.12.refs_0_, bf16[128,512]{1,0:T(8,128)(2,1)S(1)} %get-tuple-element.13.refs_1_, f32[4,1,16,128]{3,2,1,0:T(8,128)S(1)} %get-tuple-element.14.refs_2_, ...), custom_call_target="tpu_custom_call" | custom-call | tf_op jit(solution)/shard_map/hand_over/pallas_call | solution.py:462
